TPU v7x, 32 devices: a whole 2x2x4 slice. The times are simulated.
32 devices in a mesh: groups: 2 (over y), src: 16 (over z, x, core).
Axes of the slice: x: 2, y: 2, z: 4, core: 2. Of those that a mesh axis runs over, the one named last changes fastest.
Arguments:
- src_points: bfloat16 [256, 64, 256], P(('groups', 'src')), parts along dimension 0, may hold values from -1.5 to 1.5
- tgt_points: bfloat16 [256, 64, 256], P(('groups', 'src')), parts along dimension 0, may hold values from -1.5 to 1.5
- g_init: float32 [256, 256], P(('groups', 'src')), parts along dimension 0, may hold values from 2 to 66
- far_src: float32 [256, 256], P(('groups', 'src')), parts along dimension 0, may hold values from 10 to 22
- far_tgt: float32 [256, 256], P(('groups', 'src')), parts along dimension 0, may hold values from -160 to -14
- cand_owner: int32 [256, 8], P(('groups', 'src')), parts along dimension 0, may hold values from 0 to 15, all different within a row; in each aligned block of 8 rows (0 to 7, 8 to 15, ...) at most 4 rows name the same one
- cand_local: int32 [256, 8], P(('groups', 'src')), parts along dimension 0, may hold values from 0 to 7
Outputs:
- src_potential: float32 [256, 256], P(('groups', 'src')), parts along dimension 0
- tgt_potential: float32 [256, 256], P(('groups', 'src')), parts along dimension 0
There are 2 independent parts, one for each index of `groups`. A program takes and returns all parts, laid end to end along the dimension named above; each array names one. Nothing has to cross between parts.
Inputs may be any that keep to these rules, and one draw needn't show every extreme that they name: `cand_owner`: each source cluster names 8 different shards; among the 8 source clusters of one device at most 4 name the same shard, and in every draw some device names some shard exactly 4 times.
All inputs are finite; a program needn't handle non-finite values.
Results may differ from a plain program's by a relative error of at most 0.0003.
Values may be sent and summed in bfloat16 or wider, within the bound.
A program may use at most 64 MiB of HBM per device.

v0:
```python
import jax
import jax.numpy as jnp
from jax import lax
from jax.sharding import PartitionSpec as P

ITERS = 2
SCALE_EPS = 0.25
KEEP_TAU = 0.8
VERY_LOW = -1e30


def half_norms(blocks):
    wide = blocks.astype(jnp.float32)
    return 0.5 * jnp.sum(wide * wide, axis=-2)


def per_device(src_points, tgt_points, g_init, far_src, far_tgt, cand_owner, cand_local):
    src_count, feature_dim, cluster_size = src_points.shape
    tgt_count = tgt_points.shape[0]
    per_cluster = cand_owner.shape[1]
    shards = lax.axis_size("src")
    capacity = max(2, min(src_count // 2, 2 * src_count * per_cluster // shards))
    requests = src_count * per_cluster
    slot_count = shards * capacity
    group_size = 4
    group_count = src_count // group_size
    owners = cand_owner.reshape(requests)
    wanted = cand_local.reshape(requests)
    onehot = (owners[:, None] == jnp.arange(shards, dtype=jnp.int32)[None, :]).astype(jnp.int32)
    earlier = jnp.cumsum(onehot, axis=0) - onehot
    within = jnp.sum(earlier * onehot, axis=1)
    slot_pos = owners * capacity + within
    request_table = jnp.full((slot_count,), -1, jnp.int32).at[slot_pos].set(wanted)
    asked_ids = lax.all_to_all(
        request_table.reshape(shards, capacity), "src", split_axis=0, concat_axis=0, tiled=True
    ).reshape(slot_count)
    safe_ids = jnp.maximum(asked_ids, 0)
    member = (asked_ids[:, None] == jnp.arange(tgt_count, dtype=jnp.int32)[None, :]).astype(
        jnp.float32
    )
    member_rows = member.T
    send_points = tgt_points[safe_ids].reshape(shards, capacity, feature_dim, cluster_size)
    src_half = half_norms(src_points)
    src_grouped = src_points.reshape(group_count, group_size, feature_dim, cluster_size)
    half_grouped = src_half.reshape(group_count, group_size, cluster_size)
    far_grouped = far_src.reshape(group_count, group_size, cluster_size)

    def tile_cost(src_block, src_norm, tgt_block, tgt_norm):
        inner = jnp.einsum(
            "gdp,gkdq->gpkq", src_block, tgt_block, preferred_element_type=jnp.float32
        )
        return src_norm[:, :, None, None] + tgt_norm[:, None, :, :] - inner

    def row_pass(blocks, block_half, req_pot):

        def row_one_group(pieces):
            src_block, src_norm, tgt_block, tgt_norm, tgt_values, far_term = pieces
            cost = tile_cost(src_block, src_norm, tgt_block, tgt_norm)
            scores = (tgt_values[:, None, :, :] - cost) / SCALE_EPS
            highest = jnp.maximum(jnp.max(scores, axis=(2, 3)), far_term)
            total = jnp.exp(far_term - highest) + jnp.sum(
                jnp.exp(scores - highest[:, :, None, None]), axis=(2, 3)
            )
            return -KEEP_TAU * SCALE_EPS * (highest + jnp.log(total))

        pieces = (
            src_grouped,
            half_grouped,
            blocks.reshape(group_count, group_size, per_cluster, feature_dim, cluster_size),
            block_half.reshape(group_count, group_size, per_cluster, cluster_size),
            req_pot.reshape(group_count, group_size, per_cluster, cluster_size),
            far_grouped,
        )
        return lax.map(row_one_group, pieces).reshape(src_count, cluster_size)

    def column_pass(blocks, block_half, src_pot):

        def column_one_group(pieces):
            src_block, src_norm, tgt_block, tgt_norm, src_values = pieces
            cost = tile_cost(src_block, src_norm, tgt_block, tgt_norm)
            scores = (src_values[:, :, None, None] - cost) / SCALE_EPS
            highest = jnp.max(scores, axis=1)
            total = jnp.sum(jnp.exp(scores - highest[:, None, :, :]), axis=1)
            return (highest, total)

        pieces = (
            src_grouped,
            half_grouped,
            blocks.reshape(group_count, group_size, per_cluster, feature_dim, cluster_size),
            block_half.reshape(group_count, group_size, per_cluster, cluster_size),
            src_pot.reshape(group_count, group_size, cluster_size),
        )
        col_high, col_total = lax.map(column_one_group, pieces)
        col_high = col_high.reshape(requests, cluster_size)
        col_total = col_total.reshape(requests, cluster_size)
        send_high = (
            jnp.full((slot_count, cluster_size), VERY_LOW, jnp.float32).at[slot_pos].set(col_high)
        )
        send_total = jnp.zeros((slot_count, cluster_size), jnp.float32).at[slot_pos].set(col_total)
        back_high, back_total = (
            lax.all_to_all(
                send_high.reshape(shards, capacity, cluster_size),
                "src",
                split_axis=0,
                concat_axis=0,
                tiled=True,
            ),
            lax.all_to_all(
                send_total.reshape(shards, capacity, cluster_size),
                "src",
                split_axis=0,
                concat_axis=0,
                tiled=True,
            ),
        )
        back_high = back_high.reshape(slot_count, cluster_size)
        back_total = back_total.reshape(slot_count, cluster_size)

        def cluster_best(column):
            return jnp.max(jnp.where(column[:, None] > 0.5, back_high, VERY_LOW), axis=0)

        best = jnp.maximum(far_tgt, lax.map(cluster_best, member_rows))
        weights = back_total * jnp.exp(back_high - best[safe_ids])
        summed = jnp.exp(far_tgt - best) + jnp.dot(
            member_rows, weights, precision=lax.Precision.HIGHEST
        )
        return -KEEP_TAU * SCALE_EPS * (best + jnp.log(summed))

    tgt_pot = g_init
    src_pot = jnp.zeros((src_count, cluster_size), jnp.float32)
    for iteration in range(ITERS):
        flattened = lax.all_to_all(
            send_points, "src", split_axis=0, concat_axis=0, tiled=True
        ).reshape(slot_count, feature_dim, cluster_size)
        chosen = flattened[slot_pos]
        blocks = chosen
        block_half = half_norms(chosen)
        send_pot = tgt_pot[safe_ids].reshape(shards, capacity, cluster_size)
        got_pot = lax.all_to_all(send_pot, "src", split_axis=0, concat_axis=0, tiled=True)
        req_pot = got_pot.reshape(slot_count, cluster_size)[slot_pos]
        src_pot = row_pass(blocks, block_half, req_pot)
        tgt_pot = column_pass(blocks, block_half, src_pot)
    return (src_pot, tgt_pot)


def solution(mesh):
    return jax.shard_map(
        per_device,
        mesh=mesh,
        in_specs=(
            P(("groups", "src"), None, None),
            P(("groups", "src"), None, None),
            P(("groups", "src"), None),
            P(("groups", "src"), None),
            P(("groups", "src"), None),
            P(("groups", "src"), None),
            P(("groups", "src"), None),
        ),
        out_specs=(P(("groups", "src"), None), P(("groups", "src"), None)),
        check_vma=False,
    )
```

profile of v0, /device:TPU:0, one launch (start us, length us, event | category | flops | bytes accessed | tf_op | source)
XLA Modules:
  0.0 192.3 jit_solution(4724374246698592759)
XLA Ops:
  4.3 13.6 %all_to_all.45 = s32[16,1,4]{2,1,0:T(1,128)S(1)} all-to-all(s32[16,1,4]{2,1,0:T(1,128)S(1)} %bitcast.212), channel_id=1, replica_groups=mesh['groups'=2,'src'=16] {'src'}, dimensions={0} | all-to-all | bytes 512 | tf_op jit(solution)/shard_map/all_to_all | solution.py:34
  21.1 3.5 %all-to-all-start.1 = ((f32[16,4,256]{2,1,0:T(4,128)}), f32[16,4,256]{2,1,0:T(4,128)S(1)}, u32[]{:S(2)}, u32[]{:S(2)}) async-start(f32[16,4,256]{2,1,0:T(4,128)} %reshape.209), calls=%async_computation.1 | async-start | bytes 131072 | tf_op jit(solution)/shard_map/all_to_all | solution.py:139
  26.7 4.8 %all-to-all-done.1 = f32[16,4,256]{2,1,0:T(4,128)S(1)} async-done(((f32[16,4,256]{2,1,0:T(4,128)}), f32[16,4,256]{2,1,0:T(4,128)S(1)}, u32[]{:S(2)}, u32[]{:S(2)}) %all-to-all-start.1) | async-done | bytes 65568 | tf_op jit(solution)/shard_map/all_to_all | solution.py:139
  31.5 3.7 %all-to-all-start.2 = ((bf16[16,4,64,256]{3,2,1,0:T(8,128)(2,1)}), bf16[16,4,64,256]{3,2,1,0:T(8,128)(2,1)S(1)}, u32[]{:S(2)}, u32[]{:S(2)}) async-start(bf16[16,4,64,256]{3,2,1,0:T(8,128)(2,1)} %bitcast.46), calls=%async_computation.2 | async-start | bytes 4194304 | tf_op jit(solution)/shard_map/all_to_all | solution.py:132
  36.1 40.1 %all-to-all-done.2 = bf16[16,4,64,256]{3,2,1,0:T(8,128)(2,1)S(1)} async-done(((bf16[16,4,64,256]{3,2,1,0:T(8,128)(2,1)}), bf16[16,4,64,256]{3,2,1,0:T(8,128)(2,1)S(1)}, u32[]{:S(2)}, u32[]{:S(2)}) %all-to-all-start.2) | async-done | bytes 2097184 | tf_op jit(solution)/shard_map/all_to_all | solution.py:132
  77.6 2.3 %gather_fusion.3 = bf16[64,64,256]{2,1,0:T(8,128)(2,1)S(1)} fusion(bf16[64,64,256]{2,1,0:T(8,128)(2,1)} %bitcast.201, s32[1024]{0:T(1024)S(1)} %pad_clamp_fusion), kind=kCustom, calls=%fused_computation.3 | custom fusion | bytes 4194560 | tf_op jit(solution)/shard_map/gather | solution.py:135
  80.6 11.7 %while.64 = (s32[]{:T(128)}, f32[2,4,256]{2,1,0:T(4,128)S(1)}, f32[2,4,8,256]{3,2,1,0:T(8,128)S(1)}, f32[2,4,256]{2,1,0:T(4,128)S(1)}, f32[2,4,8,256]{3,2,1,0:T(...) while((s32[]{:T(128)}, f32[2,4,256]{2,1,0:T(4,128)S(1)}, ...), condition=%wide.region_8.9_spmd, body=%wide.region_5.8_spmd.sunk | while | flops 291508224 | bytes 18277484 | solution.py:74
  80.6 3.2 %fusion.69 = (f32[4,256]{1,0:T(4,128)S(1)}, f32[4,256,8,256]{1,3,2,0:T(8,128)S(1)}) fusion(f32[4,8,256]{2,1,0:T(8,128)S(1)} %get-tuple-element.552, f32[4,256]{1,0:T(4,128)S(1)} %dynamic-slice_bitcast_fusion.23, f32[4,8,256]{2,1,0:T(8,128)S(1)} %get-tuple-element.553, bf16[2,4,8,64,256]{4,3,2,1,0:T(8,128)(2,1)S(1)} %get-tuple-element.624, ...), kind=kOutput, calls=%fused_computation.15.clone.1 | convolution fusion | flops 278920192 | bytes 9643008 | tf_op jit(solution)/shard_map/while/body/eval_jaxpr/gdp,gkdq->gpkq/dot_general | solution.py:49
  83.8 2.6 %exponential_reduce_fusion.8 = f32[4,256]{1,0:T(4,128)S(1)} fusion(f32[4,256,8,256]{1,3,2,0:T(8,128)S(1)} %get-tuple-element.554, f32[4,256]{1,0:T(4,128)S(1)} %bitcast_maximum_fusion.6, f32[4,8,256]{2,1,0:T(8,128)S(1)} %get-tuple-element.552, f32[4,256]{1,0:T(4,128)S(1)} %dynamic-slice_bitcast_fusion.23, f32[4,8,256]{2,1,0:T(8,128)S(1)} %get-tuple-element.553), kind=kLoop, calls=%fused_computation.13.clone.1 | loop fusion | flops 12581888 | bytes 8466432 | tf_op jit(solution)/shard_map/while/body/eval_jaxpr/reduce_sum | solution.py:61
  86.5 3.2 %fusion.69 = (f32[4,256]{1,0:T(4,128)S(1)}, f32[4,256,8,256]{1,3,2,0:T(8,128)S(1)}) fusion(f32[4,8,256]{2,1,0:T(8,128)S(1)} %get-tuple-element.552, f32[4,256]{1,0:T(4,128)S(1)} %dynamic-slice_bitcast_fusion.23, f32[4,8,256]{2,1,0:T(8,128)S(1)} %get-tuple-element.553, bf16[2,4,8,64,256]{4,3,2,1,0:T(8,128)(2,1)S(1)} %get-tuple-element.624, ...), kind=kOutput, calls=%fused_computation.15.clone.1 | convolution fusion | flops 278920192 | bytes 9643008 | tf_op jit(solution)/shard_map/while/body/eval_jaxpr/gdp,gkdq->gpkq/dot_general | solution.py:49
  89.6 2.6 %exponential_reduce_fusion.8 = f32[4,256]{1,0:T(4,128)S(1)} fusion(f32[4,256,8,256]{1,3,2,0:T(8,128)S(1)} %get-tuple-element.554, f32[4,256]{1,0:T(4,128)S(1)} %bitcast_maximum_fusion.6, f32[4,8,256]{2,1,0:T(8,128)S(1)} %get-tuple-element.552, f32[4,256]{1,0:T(4,128)S(1)} %dynamic-slice_bitcast_fusion.23, f32[4,8,256]{2,1,0:T(8,128)S(1)} %get-tuple-element.553), kind=kLoop, calls=%fused_computation.13.clone.1 | loop fusion | flops 12581888 | bytes 8466432 | tf_op jit(solution)/shard_map/while/body/eval_jaxpr/reduce_sum | solution.py:61
  92.3 11.3 %while.65 = (s32[]{:T(128)}, f32[2,4,8,256]{3,2,1,0:T(8,128)S(1)}, f32[2,4,8,256]{3,2,1,0:T(8,128)S(1)}, f32[2,4,256]{2,1,0:T(4,128)S(1)}, f32[2,4,256]{2,1,0:T(...) while((s32[]{:T(128)}, f32[2,4,8,256]{3,2,1,0:T(8,128)S(1)}, ...), condition=%wide.region_12.13_spmd, body=%wide.region_9.12_spmd.sunk | while | flops 291487744 | bytes 18351212 | solution.py:93
  94.4 3.6 %exponential_reduce_fusion.9 = f32[4,8,256]{2,1,0:T(8,128)S(1)} fusion(f32[4,256,8,256]{3,1,2,0:T(8,128)S(1)} %get-tuple-element.564, f32[4,8,256]{2,1,0:T(8,128)S(1)} %get-tuple-element.565, f32[4,8,256]{2,1,0:T(8,128)S(1)} %dynamic-slice_bitcast_fusion.24, f32[4,256]{1,0:T(4,128)S(1)} %dynamic-slice_bitcast_fusion.25, ...), kind=kLoop, calls=%fused_computation.32.clone.1 | loop fusion | flops 12574720 | bytes 8495104 | tf_op jit(solution)/shard_map/while/body/eval_jaxpr/reduce_sum | solution.py:83
  100.0 3.6 %exponential_reduce_fusion.9 = f32[4,8,256]{2,1,0:T(8,128)S(1)} fusion(f32[4,256,8,256]{3,1,2,0:T(8,128)S(1)} %get-tuple-element.564, f32[4,8,256]{2,1,0:T(8,128)S(1)} %get-tuple-element.565, f32[4,8,256]{2,1,0:T(8,128)S(1)} %dynamic-slice_bitcast_fusion.24, f32[4,256]{1,0:T(4,128)S(1)} %dynamic-slice_bitcast_fusion.25, ...), kind=kLoop, calls=%fused_computation.32.clone.1 | loop fusion | flops 12574720 | bytes 8495104 | tf_op jit(solution)/shard_map/while/body/eval_jaxpr/reduce_sum | solution.py:83
  105.1 11.2 %all-to-all-start.3 = ((f32[16,4,256]{2,1,0:T(4,128)}), f32[16,4,256]{2,1,0:T(4,128)S(1)}, u32[]{:S(2)}, u32[]{:S(2)}) async-start(f32[16,4,256]{2,1,0:T(4,128)} %reshape.218), calls=%async_computation.3 | async-start | bytes 131072 | tf_op jit(solution)/shard_map/all_to_all | solution.py:101
  117.8 5.4 %all-to-all-done.3 = f32[16,4,256]{2,1,0:T(4,128)S(1)} async-done(((f32[16,4,256]{2,1,0:T(4,128)}), f32[16,4,256]{2,1,0:T(4,128)S(1)}, u32[]{:S(2)}, u32[]{:S(2)}) %all-to-all-start.3) | async-done | bytes 65568 | tf_op jit(solution)/shard_map/all_to_all | solution.py:101
  123.2 3.5 %all-to-all-start.4 = ((f32[16,4,256]{2,1,0:T(4,128)}), f32[16,4,256]{2,1,0:T(4,128)S(1)}, u32[]{:S(2)}, u32[]{:S(2)}) async-start(f32[16,4,256]{2,1,0:T(4,128)} %reshape.221), calls=%async_computation.4 | async-start | bytes 131072 | tf_op jit(solution)/shard_map/all_to_all | solution.py:108
  128.8 4.8 %all-to-all-done.4 = f32[16,4,256]{2,1,0:T(4,128)S(1)} async-done(((f32[16,4,256]{2,1,0:T(4,128)}), f32[16,4,256]{2,1,0:T(4,128)S(1)}, u32[]{:S(2)}, u32[]{:S(2)}) %all-to-all-start.4) | async-done | bytes 65568 | tf_op jit(solution)/shard_map/all_to_all | solution.py:108
  135.2 3.7 %all-to-all-start.5 = ((f32[16,4,256]{2,1,0:T(4,128)}), f32[16,4,256]{2,1,0:T(4,128)S(1)}, u32[]{:S(2)}, u32[]{:S(2)}) async-start(f32[16,4,256]{2,1,0:T(4,128)} %reshape.223), calls=%async_computation.5 | async-start | bytes 131072 | tf_op jit(solution)/shard_map/all_to_all | solution.py:139
  138.8 6.7 %all-to-all-done.5 = f32[16,4,256]{2,1,0:T(4,128)S(1)} async-done(((f32[16,4,256]{2,1,0:T(4,128)}), f32[16,4,256]{2,1,0:T(4,128)S(1)}, u32[]{:S(2)}, u32[]{:S(2)}) %all-to-all-start.5) | async-done | bytes 65568 | tf_op jit(solution)/shard_map/all_to_all | solution.py:139
  146.2 11.7 %while.67 = (s32[]{:T(128)}, f32[2,4,256]{2,1,0:T(4,128)S(1)}, f32[2,4,8,256]{3,2,1,0:T(8,128)S(1)}, f32[2,4,256]{2,1,0:T(4,128)S(1)}, f32[2,4,8,256]{3,2,1,0:T(...) while((s32[]{:T(128)}, f32[2,4,256]{2,1,0:T(4,128)S(1)}, ...), condition=%wide.region_21.22_spmd, body=%wide.region_18.21_spmd.sunk | while | flops 291508224 | bytes 18277484 | solution.py:74
  146.3 3.2 %fusion.72 = (f32[4,256]{1,0:T(4,128)S(1)}, f32[4,256,8,256]{1,3,2,0:T(8,128)S(1)}) fusion(f32[4,8,256]{2,1,0:T(8,128)S(1)} %get-tuple-element.580, f32[4,256]{1,0:T(4,128)S(1)} %dynamic-slice_bitcast_fusion.28, f32[4,8,256]{2,1,0:T(8,128)S(1)} %get-tuple-element.581, bf16[2,4,8,64,256]{4,3,2,1,0:T(8,128)(2,1)S(1)} %get-tuple-element.696, ...), kind=kOutput, calls=%fused_computation.50.clone.1 | convolution fusion | flops 278920192 | bytes 9643008 | tf_op jit(solution)/shard_map/while/body/eval_jaxpr/gdp,gkdq->gpkq/dot_general | solution.py:49
  149.4 2.6 %exponential_reduce_fusion.10 = f32[4,256]{1,0:T(4,128)S(1)} fusion(f32[4,256,8,256]{1,3,2,0:T(8,128)S(1)} %get-tuple-element.582, f32[4,256]{1,0:T(4,128)S(1)} %bitcast_maximum_fusion.7, f32[4,8,256]{2,1,0:T(8,128)S(1)} %get-tuple-element.580, f32[4,256]{1,0:T(4,128)S(1)} %dynamic-slice_bitcast_fusion.28, f32[4,8,256]{2,1,0:T(8,128)S(1)} %get-tuple-element.581), kind=kLoop, calls=%fused_computation.48.clone.1 | loop fusion | flops 12581888 | bytes 8466432 | tf_op jit(solution)/shard_map/while/body/eval_jaxpr/reduce_sum | solution.py:61
  152.1 3.2 %fusion.72 = (f32[4,256]{1,0:T(4,128)S(1)}, f32[4,256,8,256]{1,3,2,0:T(8,128)S(1)}) fusion(f32[4,8,256]{2,1,0:T(8,128)S(1)} %get-tuple-element.580, f32[4,256]{1,0:T(4,128)S(1)} %dynamic-slice_bitcast_fusion.28, f32[4,8,256]{2,1,0:T(8,128)S(1)} %get-tuple-element.581, bf16[2,4,8,64,256]{4,3,2,1,0:T(8,128)(2,1)S(1)} %get-tuple-element.696, ...), kind=kOutput, calls=%fused_computation.50.clone.1 | convolution fusion | flops 278920192 | bytes 9643008 | tf_op jit(solution)/shard_map/while/body/eval_jaxpr/gdp,gkdq->gpkq/dot_general | solution.py:49
  155.3 2.6 %exponential_reduce_fusion.10 = f32[4,256]{1,0:T(4,128)S(1)} fusion(f32[4,256,8,256]{1,3,2,0:T(8,128)S(1)} %get-tuple-element.582, f32[4,256]{1,0:T(4,128)S(1)} %bitcast_maximum_fusion.7, f32[4,8,256]{2,1,0:T(8,128)S(1)} %get-tuple-element.580, f32[4,256]{1,0:T(4,128)S(1)} %dynamic-slice_bitcast_fusion.28, f32[4,8,256]{2,1,0:T(8,128)S(1)} %get-tuple-element.581), kind=kLoop, calls=%fused_computation.48.clone.1 | loop fusion | flops 12581888 | bytes 8466432 | tf_op jit(solution)/shard_map/while/body/eval_jaxpr/reduce_sum | solution.py:61
  157.9 11.3 %while.68 = (s32[]{:T(128)}, f32[2,4,8,256]{3,2,1,0:T(8,128)S(1)}, f32[2,4,8,256]{3,2,1,0:T(8,128)S(1)}, f32[2,4,256]{2,1,0:T(4,128)S(1)}, f32[2,4,256]{2,1,0:T(...) while((s32[]{:T(128)}, f32[2,4,8,256]{3,2,1,0:T(8,128)S(1)}, ...), condition=%wide.region_25.26_spmd, body=%wide.region_22.25_spmd.sunk | while | flops 291487744 | bytes 18351212 | solution.py:93
  160.0 3.6 %exponential_reduce_fusion.11 = f32[4,8,256]{2,1,0:T(8,128)S(1)} fusion(f32[4,256,8,256]{3,1,2,0:T(8,128)S(1)} %get-tuple-element.592, f32[4,8,256]{2,1,0:T(8,128)S(1)} %get-tuple-element.593, f32[4,8,256]{2,1,0:T(8,128)S(1)} %dynamic-slice_bitcast_fusion.29, f32[4,256]{1,0:T(4,128)S(1)} %dynamic-slice_bitcast_fusion.30, ...), kind=kLoop, calls=%fused_computation.67.clone.1 | loop fusion | flops 12574720 | bytes 8495104 | tf_op jit(solution)/shard_map/while/body/eval_jaxpr/reduce_sum | solution.py:83
  165.6 3.6 %exponential_reduce_fusion.11 = f32[4,8,256]{2,1,0:T(8,128)S(1)} fusion(f32[4,256,8,256]{3,1,2,0:T(8,128)S(1)} %get-tuple-element.592, f32[4,8,256]{2,1,0:T(8,128)S(1)} %get-tuple-element.593, f32[4,8,256]{2,1,0:T(8,128)S(1)} %dynamic-slice_bitcast_fusion.29, f32[4,256]{1,0:T(4,128)S(1)} %dynamic-slice_bitcast_fusion.30, ...), kind=kLoop, calls=%fused_computation.67.clone.1 | loop fusion | flops 12574720 | bytes 8495104 | tf_op jit(solution)/shard_map/while/body/eval_jaxpr/reduce_sum | solution.py:83
  170.7 3.5 %all-to-all-start.6 = ((f32[16,4,256]{2,1,0:T(4,128)}), f32[16,4,256]{2,1,0:T(4,128)S(1)}, u32[]{:S(2)}, u32[]{:S(2)}) async-start(f32[16,4,256]{2,1,0:T(4,128)} %reshape.228), calls=%async_computation.6 | async-start | bytes 131072 | tf_op jit(solution)/shard_map/all_to_all | solution.py:101
  176.3 4.8 %all-to-all-done.6 = f32[16,4,256]{2,1,0:T(4,128)S(1)} async-done(((f32[16,4,256]{2,1,0:T(4,128)}), f32[16,4,256]{2,1,0:T(4,128)S(1)}, u32[]{:S(2)}, u32[]{:S(2)}) %all-to-all-start.6) | async-done | bytes 65568 | tf_op jit(solution)/shard_map/all_to_all | solution.py:101
  181.1 3.5 %all-to-all-start.7 = ((f32[16,4,256]{2,1,0:T(4,128)}), f32[16,4,256]{2,1,0:T(4,128)S(1)}, u32[]{:S(2)}, u32[]{:S(2)}) async-start(f32[16,4,256]{2,1,0:T(4,128)} %reshape.231), calls=%async_computation.7 | async-start | bytes 131072 | tf_op jit(solution)/shard_map/all_to_all | solution.py:108
  186.6 4.8 %all-to-all-done.7 = f32[16,4,256]{2,1,0:T(4,128)S(1)} async-done(((f32[16,4,256]{2,1,0:T(4,128)}), f32[16,4,256]{2,1,0:T(4,128)S(1)}, u32[]{:S(2)}, u32[]{:S(2)}) %all-to-all-start.7) | async-done | bytes 65568 | tf_op jit(solution)/shard_map/all_to_all | solution.py:108
  (155 shorter events, 36.2 us)
Async XLA Ops:
  0.6 24.0 %copy-start = (bf16[8,64,256]{2,1,0:T(8,128)(2,1)S(1)}, bf16[8,64,256]{2,1,0:T(8,128)(2,1)}, u32[]{:S(2)}) copy-start(bf16[8,64,256]{2,1,0:T(8,128)(2,1)} %param.20) | copy-start | bytes 786436
  0.6 34.6 %copy-start.2 = (bf16[8,64,256]{2,1,0:T(8,128)(2,1)S(1)}, bf16[8,64,256]{2,1,0:T(8,128)(2,1)}, u32[]{:S(2)}) copy-start(bf16[8,64,256]{2,1,0:T(8,128)(2,1)} %param.19) | copy-start | bytes 786436
  0.7 34.7 %copy-start.4 = (f32[8,256]{1,0:T(8,128)S(1)}, f32[8,256]{1,0:T(8,128)}, u32[]{:S(2)}) copy-start(f32[8,256]{1,0:T(8,128)} %param.22) | copy-start | bytes 24580
  21.1 10.4 %all-to-all-start.1 = ((f32[16,4,256]{2,1,0:T(4,128)}), f32[16,4,256]{2,1,0:T(4,128)S(1)}, u32[]{:S(2)}, u32[]{:S(2)}) async-start(f32[16,4,256]{2,1,0:T(4,128)} %reshape.209), calls=%async_computation.1 | async-start | bytes 131072 | tf_op jit(solution)/shard_map/all_to_all | solution.py:139
  31.5 44.8 %all-to-all-start.2 = ((bf16[16,4,64,256]{3,2,1,0:T(8,128)(2,1)}), bf16[16,4,64,256]{3,2,1,0:T(8,128)(2,1)S(1)}, u32[]{:S(2)}, u32[]{:S(2)}) async-start(bf16[16,4,64,256]{3,2,1,0:T(8,128)(2,1)} %bitcast.46), calls=%async_computation.2 | async-start | bytes 4194304 | tf_op jit(solution)/shard_map/all_to_all | solution.py:132
  76.2 1.4 copy-start.1
  92.3 35.8 %copy-start.3 = (f32[8,256]{1,0:T(8,128)S(1)}, f32[8,256]{1,0:T(8,128)}, u32[]{:S(2)}) copy-start(f32[8,256]{1,0:T(8,128)} %param.23) | copy-start | bytes 24580
  105.1 18.1 %all-to-all-start.3 = ((f32[16,4,256]{2,1,0:T(4,128)}), f32[16,4,256]{2,1,0:T(4,128)S(1)}, u32[]{:S(2)}, u32[]{:S(2)}) async-start(f32[16,4,256]{2,1,0:T(4,128)} %reshape.218), calls=%async_computation.3 | async-start | bytes 131072 | tf_op jit(solution)/shard_map/all_to_all | solution.py:101
  123.2 10.4 %all-to-all-start.4 = ((f32[16,4,256]{2,1,0:T(4,128)}), f32[16,4,256]{2,1,0:T(4,128)S(1)}, u32[]{:S(2)}, u32[]{:S(2)}) async-start(f32[16,4,256]{2,1,0:T(4,128)} %reshape.221), calls=%async_computation.4 | async-start | bytes 131072 | tf_op jit(solution)/shard_map/all_to_all | solution.py:108
  135.2 10.4 %all-to-all-start.5 = ((f32[16,4,256]{2,1,0:T(4,128)}), f32[16,4,256]{2,1,0:T(4,128)S(1)}, u32[]{:S(2)}, u32[]{:S(2)}) async-start(f32[16,4,256]{2,1,0:T(4,128)} %reshape.223), calls=%async_computation.5 | async-start | bytes 131072 | tf_op jit(solution)/shard_map/all_to_all | solution.py:139
  170.7 10.4 %all-to-all-start.6 = ((f32[16,4,256]{2,1,0:T(4,128)}), f32[16,4,256]{2,1,0:T(4,128)S(1)}, u32[]{:S(2)}, u32[]{:S(2)}) async-start(f32[16,4,256]{2,1,0:T(4,128)} %reshape.228), calls=%async_computation.6 | async-start | bytes 131072 | tf_op jit(solution)/shard_map/all_to_all | solution.py:101
  181.1 10.4 %all-to-all-start.7 = ((f32[16,4,256]{2,1,0:T(4,128)}), f32[16,4,256]{2,1,0:T(4,128)S(1)}, u32[]{:S(2)}, u32[]{:S(2)}) async-start(f32[16,4,256]{2,1,0:T(4,128)} %reshape.231), calls=%async_computation.7 | async-start | bytes 131072 | tf_op jit(solution)/shard_map/all_to_all | solution.py:108
where the time goes:
time: 193 us; the launch traced here: 192 us
  waiting for transfers between devices  71.4 us (37%)
  starting transfers between devices  32.6 us (17%)
  other arithmetic  28.7 us (15%)
  local copies, waits for them, and re-layouts  22.3 us (12%)
  matrix products  21.8 us (11%)
  blocking collectives  13.6 us (7%)
    all_to_all x1, waiting for transfers between devices, per_device(): lax.all_to_all(send_points, 'src', split_axis=0, concat_axis=0, tiled=True)  40.1 us
    dot_general x8, matrix products, tile_cost(): jnp.einsum('gdp,gkdq->gpkq', src_block, tgt_block, preferred_element_type...  20.7 us
    all_to_all x2, starting transfers between devices, column_pass(): lax.all_to_all(send_high.reshape(shards, capacity, cluster_size), 'src',...  14.7 us
    reduce_sum x4, other arithmetic, column_one_group(): total = jnp.sum(jnp.exp(scores - highest[:, None, :, :]), axis=1)  14.2 us
    all_to_all x1, blocking collectives, per_device(): lax.all_to_all(request_table.reshape(shards, capacity), 'src', split_axis...  13.6 us
    all_to_all x2, waiting for transfers between devices, per_device(): lax.all_to_all(send_pot, 'src', split_axis=0, concat_axis=0, tiled=True)  11.5 us
    reduce_sum x4, other arithmetic, row_one_group(): jnp.sum(jnp.exp(scores - highest[:, :, None, None]), axis=(2, 3))  10.2 us
    all_to_all x2, waiting for transfers between devices, column_pass(): lax.all_to_all(send_high.reshape(shards, capacity, cluster_size), 'src',...  10.2 us
  transfers between devices with their start and end apart: 7, of which 7 were waited for; matrix products, arithmetic and copies ran while one was open for 5% of the time, Pallas kernels for 0%

commit v1 on v0

--- a/solution.py
+++ b/solution.py
@@ -7,6 +7,18 @@
 SCALE_EPS = 0.25
 KEEP_TAU = 0.8
 VERY_LOW = -1e30
+
+
+def sent_to_each(x, axis, split, join):
+    ways, here = (lax.axis_size(axis), lax.axis_index(axis))
+    width = x.shape[split] // ways
+    turned = jnp.roll(x, -here * width, axis=split)
+    got = [lax.slice_in_dim(turned, 0, width, axis=split)]
+    for far in range(1, ways):
+        sent = lax.slice_in_dim(turned, far * width, (far + 1) * width, axis=split)
+        got.append(lax.ppermute(sent, axis, [(d, (d + far) % ways) for d in range(ways)]))
+    line = jnp.concatenate(got[::-1], axis=join)
+    return jnp.roll(line, (here + 1) * got[0].shape[join], axis=join)
 
 
 def half_norms(blocks):
@@ -98,13 +110,7 @@
         )
         send_total = jnp.zeros((slot_count, cluster_size), jnp.float32).at[slot_pos].set(col_total)
         back_high, back_total = (
-            lax.all_to_all(
-                send_high.reshape(shards, capacity, cluster_size),
-                "src",
-                split_axis=0,
-                concat_axis=0,
-                tiled=True,
-            ),
+            sent_to_each(send_high.reshape(shards, capacity, cluster_size), "src", 0, 0),
             lax.all_to_all(
                 send_total.reshape(shards, capacity, cluster_size),
                 "src",

time: 193 us -> 217 us (1.12)
  starting transfers between devices: 32.6 us -> 66 us
  waiting for transfers between devices: 71.4 us -> 63 us
    ppermute x0 -> x30, starting transfers between devices: none -> 45.5 us  [sent_to_each(): lax.ppermute(sent, axis, [(d, (d + far) % ways) for d in range(ways)])]
    all_to_all x2 -> x0, starting transfers between devices: 14.7 us -> none  [column_pass(): lax.all_to_all(send_high.reshape(shards, capacity, cluster_size), 'src',...]
    ppermute x0 -> x30, waiting for transfers between devices: none -> 11.4 us  [sent_to_each(): lax.ppermute(sent, axis, [(d, (d + far) % ways) for d in range(ways)])]
    all_to_all x2 -> x0, waiting for transfers between devices: 10.2 us -> none  [column_pass(): lax.all_to_all(send_high.reshape(shards, capacity, cluster_size), 'src',...]
    all_to_all x2, waiting for transfers between devices: 9.59 us -> 0.01 us  [column_pass(): lax.all_to_all(send_total.reshape(shards, capacity, cluster_size), 'src',...]
    all_to_all x2, starting transfers between devices: 6.98 us -> 9.58 us  [column_pass(): lax.all_to_all(send_total.reshape(shards, capacity, cluster_size), 'src',...]
  transfers between devices with their start and end apart: 7 -> 35, of which waited for: 7 -> 11; matrix products, arithmetic and copies ran while one was open for 5% -> 5% of each run, Pallas kernels for 0% -> 0%
where the time goes in v1:
time: 217 us
  starting transfers between devices  66 us (30%)
  waiting for transfers between devices  63 us (29%)
  other arithmetic  29 us (13%)
  matrix products  21.8 us (10%)
  local copies, waits for them, and re-layouts  21.3 us (10%)
  blocking collectives  13.6 us (6%)
    ppermute x30, starting transfers between devices, sent_to_each(): lax.ppermute(sent, axis, [(d, (d + far) % ways) for d in range(ways)])  45.5 us
    all_to_all x1, waiting for transfers between devices, per_device(): lax.all_to_all(send_points, 'src', split_axis=0, concat_axis=0, tiled=True)  40.1 us
    dot_general x8, matrix products, tile_cost(): jnp.einsum('gdp,gkdq->gpkq', src_block, tgt_block, preferred_element_type...  20.7 us
    reduce_sum x4, other arithmetic, column_one_group(): total = jnp.sum(jnp.exp(scores - highest[:, None, :, :]), axis=1)  14.2 us
    all_to_all x1, blocking collectives, per_device(): lax.all_to_all(request_table.reshape(shards, capacity), 'src', split_axis...  13.6 us
    all_to_all x2, waiting for transfers between devices, per_device(): lax.all_to_all(send_pot, 'src', split_axis=0, concat_axis=0, tiled=True)  11.5 us
    ppermute x30, waiting for transfers between devices, sent_to_each(): lax.ppermute(sent, axis, [(d, (d + far) % ways) for d in range(ways)])  11.4 us
    reduce_sum x4, other arithmetic, row_one_group(): jnp.sum(jnp.exp(scores - highest[:, :, None, None]), axis=(2, 3))  10.2 us
  transfers between devices with their start and end apart: 35, of which 11 were waited for; matrix products, arithmetic and copies ran while one was open for 5% of the time, Pallas kernels for 0%

profile of v1, /device:TPU:0, one launch (start us, length us, event | category | flops | bytes accessed | tf_op | source)
XLA Modules:
  0.0 216.8 jit_solution(17004187132619103921)
XLA Ops:
  4.3 13.6 %all_to_all.35 = s32[16,1,4]{2,1,0:T(1,128)S(1)} all-to-all(s32[16,1,4]{2,1,0:T(1,128)S(1)} %bitcast.212), channel_id=1, replica_groups=mesh['groups'=2,'src'=16] {'src'}, dimensions={0} | all-to-all | bytes 512 | tf_op jit(solution)/shard_map/all_to_all | solution.py:46
  21.1 3.5 %all-to-all-start.1 = ((f32[16,4,256]{2,1,0:T(4,128)}), f32[16,4,256]{2,1,0:T(4,128)S(1)}, u32[]{:S(2)}, u32[]{:S(2)}) async-start(f32[16,4,256]{2,1,0:T(4,128)} %reshape.209), calls=%async_computation.1 | async-start | bytes 131072 | tf_op jit(solution)/shard_map/all_to_all | solution.py:145
  26.6 4.8 %all-to-all-done.1 = f32[16,4,256]{2,1,0:T(4,128)S(1)} async-done(((f32[16,4,256]{2,1,0:T(4,128)}), f32[16,4,256]{2,1,0:T(4,128)S(1)}, u32[]{:S(2)}, u32[]{:S(2)}) %all-to-all-start.1) | async-done | bytes 65568 | tf_op jit(solution)/shard_map/all_to_all | solution.py:145
  31.5 3.7 %all-to-all-start.2 = ((bf16[16,4,64,256]{3,2,1,0:T(8,128)(2,1)}), bf16[16,4,64,256]{3,2,1,0:T(8,128)(2,1)S(1)}, u32[]{:S(2)}, u32[]{:S(2)}) async-start(bf16[16,4,64,256]{3,2,1,0:T(8,128)(2,1)} %bitcast.46), calls=%async_computation.2 | async-start | bytes 4194304 | tf_op jit(solution)/shard_map/all_to_all | solution.py:138
  36.2 40.1 %all-to-all-done.2 = bf16[16,4,64,256]{3,2,1,0:T(8,128)(2,1)S(1)} async-done(((bf16[16,4,64,256]{3,2,1,0:T(8,128)(2,1)}), bf16[16,4,64,256]{3,2,1,0:T(8,128)(2,1)S(1)}, u32[]{:S(2)}, u32[]{:S(2)}) %all-to-all-start.2) | async-done | bytes 2097184 | tf_op jit(solution)/shard_map/all_to_all | solution.py:138
  80.6 11.7 %while.64 = (s32[]{:T(128)}, f32[2,4,256]{2,1,0:T(4,128)S(1)}, f32[2,4,8,256]{3,2,1,0:T(8,128)S(1)}, f32[2,4,256]{2,1,0:T(4,128)S(1)}, f32[2,4,8,256]{3,2,1,0:T(...) while((s32[]{:T(128)}, f32[2,4,256]{2,1,0:T(4,128)S(1)}, ...), condition=%wide.region_8.9_spmd, body=%wide.region_5.8_spmd.sunk | while | flops 291508224 | bytes 18277484 | solution.py:86
  80.6 3.2 %fusion.75 = (f32[4,256]{1,0:T(4,128)S(1)}, f32[4,256,8,256]{1,3,2,0:T(8,128)S(1)}) fusion(f32[4,8,256]{2,1,0:T(8,128)S(1)} %get-tuple-element.583, f32[4,256]{1,0:T(4,128)S(1)} %dynamic-slice_bitcast_fusion.23, f32[4,8,256]{2,1,0:T(8,128)S(1)} %get-tuple-element.584, bf16[2,4,8,64,256]{4,3,2,1,0:T(8,128)(2,1)S(1)} %get-tuple-element.655, ...), kind=kOutput, calls=%fused_computation.15.clone.1 | convolution fusion | flops 278920192 | bytes 9643008 | tf_op jit(solution)/shard_map/while/body/eval_jaxpr/gdp,gkdq->gpkq/dot_general | solution.py:61
  83.8 2.6 %exponential_reduce_fusion.8 = f32[4,256]{1,0:T(4,128)S(1)} fusion(f32[4,256,8,256]{1,3,2,0:T(8,128)S(1)} %get-tuple-element.585, f32[4,256]{1,0:T(4,128)S(1)} %bitcast_maximum_fusion.6, f32[4,8,256]{2,1,0:T(8,128)S(1)} %get-tuple-element.583, f32[4,256]{1,0:T(4,128)S(1)} %dynamic-slice_bitcast_fusion.23, f32[4,8,256]{2,1,0:T(8,128)S(1)} %get-tuple-element.584), kind=kLoop, calls=%fused_computation.13.clone.1 | loop fusion | flops 12581888 | bytes 8466432 | tf_op jit(solution)/shard_map/while/body/eval_jaxpr/reduce_sum | solution.py:73
  86.4 3.2 %fusion.75 = (f32[4,256]{1,0:T(4,128)S(1)}, f32[4,256,8,256]{1,3,2,0:T(8,128)S(1)}) fusion(f32[4,8,256]{2,1,0:T(8,128)S(1)} %get-tuple-element.583, f32[4,256]{1,0:T(4,128)S(1)} %dynamic-slice_bitcast_fusion.23, f32[4,8,256]{2,1,0:T(8,128)S(1)} %get-tuple-element.584, bf16[2,4,8,64,256]{4,3,2,1,0:T(8,128)(2,1)S(1)} %get-tuple-element.655, ...), kind=kOutput, calls=%fused_computation.15.clone.1 | convolution fusion | flops 278920192 | bytes 9643008 | tf_op jit(solution)/shard_map/while/body/eval_jaxpr/gdp,gkdq->gpkq/dot_general | solution.py:61
  89.6 2.6 %exponential_reduce_fusion.8 = f32[4,256]{1,0:T(4,128)S(1)} fusion(f32[4,256,8,256]{1,3,2,0:T(8,128)S(1)} %get-tuple-element.585, f32[4,256]{1,0:T(4,128)S(1)} %bitcast_maximum_fusion.6, f32[4,8,256]{2,1,0:T(8,128)S(1)} %get-tuple-element.583, f32[4,256]{1,0:T(4,128)S(1)} %dynamic-slice_bitcast_fusion.23, f32[4,8,256]{2,1,0:T(8,128)S(1)} %get-tuple-element.584), kind=kLoop, calls=%fused_computation.13.clone.1 | loop fusion | flops 12581888 | bytes 8466432 | tf_op jit(solution)/shard_map/while/body/eval_jaxpr/reduce_sum | solution.py:73
  92.3 11.3 %while.65 = (s32[]{:T(128)}, f32[2,4,8,256]{3,2,1,0:T(8,128)S(1)}, f32[2,4,8,256]{3,2,1,0:T(8,128)S(1)}, f32[2,4,256]{2,1,0:T(4,128)S(1)}, f32[2,4,256]{2,1,0:T(...) while((s32[]{:T(128)}, f32[2,4,8,256]{3,2,1,0:T(8,128)S(1)}, ...), condition=%wide.region_12.13_spmd, body=%wide.region_9.12_spmd.sunk | while | flops 291487744 | bytes 18351212 | solution.py:105
  94.3 3.6 %exponential_reduce_fusion.9 = f32[4,8,256]{2,1,0:T(8,128)S(1)} fusion(f32[4,256,8,256]{3,1,2,0:T(8,128)S(1)} %get-tuple-element.595, f32[4,8,256]{2,1,0:T(8,128)S(1)} %get-tuple-element.596, f32[4,8,256]{2,1,0:T(8,128)S(1)} %dynamic-slice_bitcast_fusion.24, f32[4,256]{1,0:T(4,128)S(1)} %dynamic-slice_bitcast_fusion.25, ...), kind=kLoop, calls=%fused_computation.32.clone.1 | loop fusion | flops 12574720 | bytes 8495104 | tf_op jit(solution)/shard_map/while/body/eval_jaxpr/reduce_sum | solution.py:95
  100.0 3.6 %exponential_reduce_fusion.9 = f32[4,8,256]{2,1,0:T(8,128)S(1)} fusion(f32[4,256,8,256]{3,1,2,0:T(8,128)S(1)} %get-tuple-element.595, f32[4,8,256]{2,1,0:T(8,128)S(1)} %get-tuple-element.596, f32[4,8,256]{2,1,0:T(8,128)S(1)} %dynamic-slice_bitcast_fusion.24, f32[4,256]{1,0:T(4,128)S(1)} %dynamic-slice_bitcast_fusion.25, ...), kind=kLoop, calls=%fused_computation.32.clone.1 | loop fusion | flops 12574720 | bytes 8495104 | tf_op jit(solution)/shard_map/while/body/eval_jaxpr/reduce_sum | solution.py:95
  104.5 9.8 %collective-permute-start = (f32[1,4,256]{2,1,0:T(4,128)S(1)}, f32[1,4,256]{2,1,0:T(4,128)S(1)}, u32[]{:S(2)}, u32[]{:S(2)}) collective-permute-start(f32[1,4,256]{2,1,0:T(4,128)S(1)} %get-tuple-element.352), channel_id=1, source_target_pairs={{0,15},{1,0},{2,1},{3,2},{4,3},{5,4},{6,5},{7,6},{8,7},{9,8},{10,9... | collective-permute-start | bytes 12296 | tf_op jit(solution)/shard_map/ppermute | solution.py:19
  117.8 6.1 %all-to-all-start.3 = ((f32[16,4,256]{2,1,0:T(4,128)}), f32[16,4,256]{2,1,0:T(4,128)S(1)}, u32[]{:S(2)}, u32[]{:S(2)}) async-start(f32[16,4,256]{2,1,0:T(4,128)} %reshape.221), calls=%async_computation.3 | async-start | bytes 131072 | tf_op jit(solution)/shard_map/all_to_all | solution.py:114
  123.9 3.8 %collective-permute-start.5 = (f32[1,4,256]{2,1,0:T(4,128)S(1)}, f32[1,4,256]{2,1,0:T(4,128)S(1)}, u32[]{:S(2)}, u32[]{:S(2)}) collective-permute-start(f32[1,4,256]{2,1,0:T(4,128)S(1)} %get-tuple-element.347), channel_id=1, source_target_pairs={{0,10},{1,11},{2,12},{3,13},{4,14},{5,15},{6,0},{7,1},{8,2},{9,3},... | collective-permute-start | bytes 12296 | tf_op jit(solution)/shard_map/ppermute | solution.py:19
  140.9 3.0 %collective-permute-done.13 = f32[1,4,256]{2,1,0:T(4,128)S(1)} collective-permute-done((f32[1,4,256]{2,1,0:T(4,128)S(1)}, f32[1,4,256]{2,1,0:T(4,128)S(1)}, u32[]{:S(2)}, u32[]{:S(2)}) %collective-permute-start.13) | collective-permute-done | bytes 4128 | tf_op jit(solution)/shard_map/ppermute | solution.py:19
  147.9 3.7 %all-to-all-start.4 = ((f32[16,4,256]{2,1,0:T(4,128)}), f32[16,4,256]{2,1,0:T(4,128)S(1)}, u32[]{:S(2)}, u32[]{:S(2)}) async-start(f32[16,4,256]{2,1,0:T(4,128)} %reshape.223), calls=%async_computation.4 | async-start | bytes 131072 | tf_op jit(solution)/shard_map/all_to_all | solution.py:145
  151.6 6.7 %all-to-all-done.4 = f32[16,4,256]{2,1,0:T(4,128)S(1)} async-done(((f32[16,4,256]{2,1,0:T(4,128)}), f32[16,4,256]{2,1,0:T(4,128)S(1)}, u32[]{:S(2)}, u32[]{:S(2)}) %all-to-all-start.4) | async-done | bytes 65568 | tf_op jit(solution)/shard_map/all_to_all | solution.py:145
  159.0 11.7 %while.67 = (s32[]{:T(128)}, f32[2,4,256]{2,1,0:T(4,128)S(1)}, f32[2,4,8,256]{3,2,1,0:T(8,128)S(1)}, f32[2,4,256]{2,1,0:T(4,128)S(1)}, f32[2,4,8,256]{3,2,1,0:T(...) while((s32[]{:T(128)}, f32[2,4,256]{2,1,0:T(4,128)S(1)}, ...), condition=%wide.region_21.23_spmd, body=%wide.region_18.22_spmd.sunk | while | flops 291508224 | bytes 18277484 | solution.py:86
  159.0 3.2 %fusion.78 = (f32[4,256]{1,0:T(4,128)S(1)}, f32[4,256,8,256]{1,3,2,0:T(8,128)S(1)}) fusion(f32[4,8,256]{2,1,0:T(8,128)S(1)} %get-tuple-element.611, f32[4,256]{1,0:T(4,128)S(1)} %dynamic-slice_bitcast_fusion.28, f32[4,8,256]{2,1,0:T(8,128)S(1)} %get-tuple-element.612, bf16[2,4,8,64,256]{4,3,2,1,0:T(8,128)(2,1)S(1)} %get-tuple-element.727, ...), kind=kOutput, calls=%fused_computation.50.clone.1 | convolution fusion | flops 278920192 | bytes 9643008 | tf_op jit(solution)/shard_map/while/body/eval_jaxpr/gdp,gkdq->gpkq/dot_general | solution.py:61
  162.2 2.6 %exponential_reduce_fusion.10 = f32[4,256]{1,0:T(4,128)S(1)} fusion(f32[4,256,8,256]{1,3,2,0:T(8,128)S(1)} %get-tuple-element.613, f32[4,256]{1,0:T(4,128)S(1)} %bitcast_maximum_fusion.7, f32[4,8,256]{2,1,0:T(8,128)S(1)} %get-tuple-element.611, f32[4,256]{1,0:T(4,128)S(1)} %dynamic-slice_bitcast_fusion.28, f32[4,8,256]{2,1,0:T(8,128)S(1)} %get-tuple-element.612), kind=kLoop, calls=%fused_computation.48.clone.1 | loop fusion | flops 12581888 | bytes 8466432 | tf_op jit(solution)/shard_map/while/body/eval_jaxpr/reduce_sum | solution.py:73
  164.8 3.2 %fusion.78 = (f32[4,256]{1,0:T(4,128)S(1)}, f32[4,256,8,256]{1,3,2,0:T(8,128)S(1)}) fusion(f32[4,8,256]{2,1,0:T(8,128)S(1)} %get-tuple-element.611, f32[4,256]{1,0:T(4,128)S(1)} %dynamic-slice_bitcast_fusion.28, f32[4,8,256]{2,1,0:T(8,128)S(1)} %get-tuple-element.612, bf16[2,4,8,64,256]{4,3,2,1,0:T(8,128)(2,1)S(1)} %get-tuple-element.727, ...), kind=kOutput, calls=%fused_computation.50.clone.1 | convolution fusion | flops 278920192 | bytes 9643008 | tf_op jit(solution)/shard_map/while/body/eval_jaxpr/gdp,gkdq->gpkq/dot_general | solution.py:61
  168.0 2.6 %exponential_reduce_fusion.10 = f32[4,256]{1,0:T(4,128)S(1)} fusion(f32[4,256,8,256]{1,3,2,0:T(8,128)S(1)} %get-tuple-element.613, f32[4,256]{1,0:T(4,128)S(1)} %bitcast_maximum_fusion.7, f32[4,8,256]{2,1,0:T(8,128)S(1)} %get-tuple-element.611, f32[4,256]{1,0:T(4,128)S(1)} %dynamic-slice_bitcast_fusion.28, f32[4,8,256]{2,1,0:T(8,128)S(1)} %get-tuple-element.612), kind=kLoop, calls=%fused_computation.48.clone.1 | loop fusion | flops 12581888 | bytes 8466432 | tf_op jit(solution)/shard_map/while/body/eval_jaxpr/reduce_sum | solution.py:73
  170.6 11.3 %while.68 = (s32[]{:T(128)}, f32[2,4,8,256]{3,2,1,0:T(8,128)S(1)}, f32[2,4,8,256]{3,2,1,0:T(8,128)S(1)}, f32[2,4,256]{2,1,0:T(4,128)S(1)}, f32[2,4,256]{2,1,0:T(...) while((s32[]{:T(128)}, f32[2,4,8,256]{3,2,1,0:T(8,128)S(1)}, ...), condition=%wide.region_25.27_spmd, body=%wide.region_22.26_spmd.sunk | while | flops 291487744 | bytes 18351212 | solution.py:105
  172.7 3.6 %exponential_reduce_fusion.11 = f32[4,8,256]{2,1,0:T(8,128)S(1)} fusion(f32[4,256,8,256]{3,1,2,0:T(8,128)S(1)} %get-tuple-element.623, f32[4,8,256]{2,1,0:T(8,128)S(1)} %get-tuple-element.624, f32[4,8,256]{2,1,0:T(8,128)S(1)} %dynamic-slice_bitcast_fusion.29, f32[4,256]{1,0:T(4,128)S(1)} %dynamic-slice_bitcast_fusion.30, ...), kind=kLoop, calls=%fused_computation.67.clone.1 | loop fusion | flops 12574720 | bytes 8495104 | tf_op jit(solution)/shard_map/while/body/eval_jaxpr/reduce_sum | solution.py:95
  178.4 3.6 %exponential_reduce_fusion.11 = f32[4,8,256]{2,1,0:T(8,128)S(1)} fusion(f32[4,256,8,256]{3,1,2,0:T(8,128)S(1)} %get-tuple-element.623, f32[4,8,256]{2,1,0:T(8,128)S(1)} %get-tuple-element.624, f32[4,8,256]{2,1,0:T(8,128)S(1)} %dynamic-slice_bitcast_fusion.29, f32[4,256]{1,0:T(4,128)S(1)} %dynamic-slice_bitcast_fusion.30, ...), kind=kLoop, calls=%fused_computation.67.clone.1 | loop fusion | flops 12574720 | bytes 8495104 | tf_op jit(solution)/shard_map/while/body/eval_jaxpr/reduce_sum | solution.py:95
  190.1 3.5 %all-to-all-start.5 = ((f32[16,4,256]{2,1,0:T(4,128)}), f32[16,4,256]{2,1,0:T(4,128)S(1)}, u32[]{:S(2)}, u32[]{:S(2)}) async-start(f32[16,4,256]{2,1,0:T(4,128)} %reshape.231), calls=%async_computation.5 | async-start | bytes 131072 | tf_op jit(solution)/shard_map/all_to_all | solution.py:114
  193.6 3.7 %collective-permute-start.20 = (f32[1,4,256]{2,1,0:T(4,128)S(1)}, f32[1,4,256]{2,1,0:T(4,128)S(1)}, u32[]{:S(2)}, u32[]{:S(2)}) collective-permute-start(f32[1,4,256]{2,1,0:T(4,128)S(1)} %get-tuple-element.332), channel_id=1, source_target_pairs={{0,10},{1,11},{2,12},{3,13},{4,14},{5,15},{6,0},{7,1},{8,2},{9,3},... | collective-permute-start | bytes 12296 | tf_op jit(solution)/shard_map/ppermute | solution.py:19
  197.4 2.4 %collective-permute-start.22 = (f32[1,4,256]{2,1,0:T(4,128)S(1)}, f32[1,4,256]{2,1,0:T(4,128)S(1)}, u32[]{:S(2)}, u32[]{:S(2)}) collective-permute-start(f32[1,4,256]{2,1,0:T(4,128)S(1)} %get-tuple-element.330), channel_id=1, source_target_pairs={{0,8},{1,9},{2,10},{3,11},{4,12},{5,13},{6,14},{7,15},{8,0},{9,1},... | collective-permute-start | bytes 12296 | tf_op jit(solution)/shard_map/ppermute | solution.py:19
  200.3 2.4 %collective-permute-start.24 = (f32[1,4,256]{2,1,0:T(4,128)S(1)}, f32[1,4,256]{2,1,0:T(4,128)S(1)}, u32[]{:S(2)}, u32[]{:S(2)}) collective-permute-start(f32[1,4,256]{2,1,0:T(4,128)S(1)} %get-tuple-element.328), channel_id=1, source_target_pairs={{0,6},{1,7},{2,8},{3,9},{4,10},{5,11},{6,12},{7,13},{8,14},{9,15},... | collective-permute-start | bytes 12296 | tf_op jit(solution)/shard_map/ppermute | solution.py:19
  210.6 3.0 %collective-permute-done.28 = f32[1,4,256]{2,1,0:T(4,128)S(1)} collective-permute-done((f32[1,4,256]{2,1,0:T(4,128)S(1)}, f32[1,4,256]{2,1,0:T(4,128)S(1)}, u32[]{:S(2)}, u32[]{:S(2)}) %collective-permute-start.28) | collective-permute-done | bytes 4128 | tf_op jit(solution)/shard_map/ppermute | solution.py:19
  (249 shorter events, 66.6 us)
Async XLA Ops:
  21.1 10.4 %all-to-all-start.1 = ((f32[16,4,256]{2,1,0:T(4,128)}), f32[16,4,256]{2,1,0:T(4,128)S(1)}, u32[]{:S(2)}, u32[]{:S(2)}) async-start(f32[16,4,256]{2,1,0:T(4,128)} %reshape.209), calls=%async_computation.1 | async-start | bytes 131072 | tf_op jit(solution)/shard_map/all_to_all | solution.py:145
  31.5 44.8 %all-to-all-start.2 = ((bf16[16,4,64,256]{3,2,1,0:T(8,128)(2,1)}), bf16[16,4,64,256]{3,2,1,0:T(8,128)(2,1)S(1)}, u32[]{:S(2)}, u32[]{:S(2)}) async-start(bf16[16,4,64,256]{3,2,1,0:T(8,128)(2,1)} %bitcast.46), calls=%async_computation.2 | async-start | bytes 4194304 | tf_op jit(solution)/shard_map/all_to_all | solution.py:138
  104.5 19.4 %collective-permute-start = (f32[1,4,256]{2,1,0:T(4,128)S(1)}, f32[1,4,256]{2,1,0:T(4,128)S(1)}, u32[]{:S(2)}, u32[]{:S(2)}) collective-permute-start(f32[1,4,256]{2,1,0:T(4,128)S(1)} %get-tuple-element.352), channel_id=1, source_target_pairs={{0,15},{1,0},{2,1},{3,2},{4,3},{5,4},{6,5},{7,6},{8,7},{9,8},{10,9... | collective-permute-start | bytes 12296 | tf_op jit(solution)/shard_map/ppermute | solution.py:19
  114.3 13.4 %collective-permute-start.1 = (f32[1,4,256]{2,1,0:T(4,128)S(1)}, f32[1,4,256]{2,1,0:T(4,128)S(1)}, u32[]{:S(2)}, u32[]{:S(2)}) collective-permute-start(f32[1,4,256]{2,1,0:T(4,128)S(1)} %get-tuple-element.351), channel_id=1, source_target_pairs={{0,14},{1,15},{2,0},{3,1},{4,2},{5,3},{6,4},{7,5},{8,6},{9,7},{10,... | collective-permute-start | bytes 12296 | tf_op jit(solution)/shard_map/ppermute | solution.py:19
  114.5 13.3 %collective-permute-start.2 = (f32[1,4,256]{2,1,0:T(4,128)S(1)}, f32[1,4,256]{2,1,0:T(4,128)S(1)}, u32[]{:S(2)}, u32[]{:S(2)}) collective-permute-start(f32[1,4,256]{2,1,0:T(4,128)S(1)} %get-tuple-element.350), channel_id=1, source_target_pairs={{0,13},{1,14},{2,15},{3,0},{4,1},{5,2},{6,3},{7,4},{8,5},{9,6},{10... | collective-permute-start | bytes 12296 | tf_op jit(solution)/shard_map/ppermute | solution.py:19
  114.5 15.7 %collective-permute-start.3 = (f32[1,4,256]{2,1,0:T(4,128)S(1)}, f32[1,4,256]{2,1,0:T(4,128)S(1)}, u32[]{:S(2)}, u32[]{:S(2)}) collective-permute-start(f32[1,4,256]{2,1,0:T(4,128)S(1)} %get-tuple-element.349), channel_id=1, source_target_pairs={{0,12},{1,13},{2,14},{3,15},{4,0},{5,1},{6,2},{7,3},{8,4},{9,5},{1... | collective-permute-start | bytes 12296 | tf_op jit(solution)/shard_map/ppermute | solution.py:19
  116.4 14.3 %collective-permute-start.4 = (f32[1,4,256]{2,1,0:T(4,128)S(1)}, f32[1,4,256]{2,1,0:T(4,128)S(1)}, u32[]{:S(2)}, u32[]{:S(2)}) collective-permute-start(f32[1,4,256]{2,1,0:T(4,128)S(1)} %get-tuple-element.348), channel_id=1, source_target_pairs={{0,11},{1,12},{2,13},{3,14},{4,15},{5,0},{6,1},{7,2},{8,3},{9,4},{... | collective-permute-start | bytes 12296 | tf_op jit(solution)/shard_map/ppermute | solution.py:19
  117.8 28.4 %all-to-all-start.3 = ((f32[16,4,256]{2,1,0:T(4,128)}), f32[16,4,256]{2,1,0:T(4,128)S(1)}, u32[]{:S(2)}, u32[]{:S(2)}) async-start(f32[16,4,256]{2,1,0:T(4,128)} %reshape.221), calls=%async_computation.3 | async-start | bytes 131072 | tf_op jit(solution)/shard_map/all_to_all | solution.py:114
  123.9 9.1 %collective-permute-start.5 = (f32[1,4,256]{2,1,0:T(4,128)S(1)}, f32[1,4,256]{2,1,0:T(4,128)S(1)}, u32[]{:S(2)}, u32[]{:S(2)}) collective-permute-start(f32[1,4,256]{2,1,0:T(4,128)S(1)} %get-tuple-element.347), channel_id=1, source_target_pairs={{0,10},{1,11},{2,12},{3,13},{4,14},{5,15},{6,0},{7,1},{8,2},{9,3},... | collective-permute-start | bytes 12296 | tf_op jit(solution)/shard_map/ppermute | solution.py:19
  127.7 6.3 %collective-permute-start.6 = (f32[1,4,256]{2,1,0:T(4,128)S(1)}, f32[1,4,256]{2,1,0:T(4,128)S(1)}, u32[]{:S(2)}, u32[]{:S(2)}) collective-permute-start(f32[1,4,256]{2,1,0:T(4,128)S(1)} %get-tuple-element.346), channel_id=1, source_target_pairs={{0,9},{1,10},{2,11},{3,12},{4,13},{5,14},{6,15},{7,0},{8,1},{9,2},... | collective-permute-start | bytes 12296 | tf_op jit(solution)/shard_map/ppermute | solution.py:19
  127.8 7.7 %collective-permute-start.7 = (f32[1,4,256]{2,1,0:T(4,128)S(1)}, f32[1,4,256]{2,1,0:T(4,128)S(1)}, u32[]{:S(2)}, u32[]{:S(2)}) collective-permute-start(f32[1,4,256]{2,1,0:T(4,128)S(1)} %get-tuple-element.345), channel_id=1, source_target_pairs={{0,8},{1,9},{2,10},{3,11},{4,12},{5,13},{6,14},{7,15},{8,0},{9,1},... | collective-permute-start | bytes 12296 | tf_op jit(solution)/shard_map/ppermute | solution.py:19
  130.1 7.5 %collective-permute-start.8 = (f32[1,4,256]{2,1,0:T(4,128)S(1)}, f32[1,4,256]{2,1,0:T(4,128)S(1)}, u32[]{:S(2)}, u32[]{:S(2)}) collective-permute-start(f32[1,4,256]{2,1,0:T(4,128)S(1)} %get-tuple-element.344), channel_id=1, source_target_pairs={{0,7},{1,8},{2,9},{3,10},{4,11},{5,12},{6,13},{7,14},{8,15},{9,0},... | collective-permute-start | bytes 12296 | tf_op jit(solution)/shard_map/ppermute | solution.py:19
  130.7 7.7 %collective-permute-start.9 = (f32[1,4,256]{2,1,0:T(4,128)S(1)}, f32[1,4,256]{2,1,0:T(4,128)S(1)}, u32[]{:S(2)}, u32[]{:S(2)}) collective-permute-start(f32[1,4,256]{2,1,0:T(4,128)S(1)} %get-tuple-element.343), channel_id=1, source_target_pairs={{0,6},{1,7},{2,8},{3,9},{4,10},{5,11},{6,12},{7,13},{8,14},{9,15},... | collective-permute-start | bytes 12296 | tf_op jit(solution)/shard_map/ppermute | solution.py:19
  134.0 5.4 %collective-permute-start.11 = (f32[1,4,256]{2,1,0:T(4,128)S(1)}, f32[1,4,256]{2,1,0:T(4,128)S(1)}, u32[]{:S(2)}, u32[]{:S(2)}) collective-permute-start(f32[1,4,256]{2,1,0:T(4,128)S(1)} %get-tuple-element.341), channel_id=1, source_target_pairs={{0,4},{1,5},{2,6},{3,7},{4,8},{5,9},{6,10},{7,11},{8,12},{9,13},{1... | collective-permute-start | bytes 12296 | tf_op jit(solution)/shard_map/ppermute | solution.py:19
  135.5 5.4 %collective-permute-start.12 = (f32[1,4,256]{2,1,0:T(4,128)S(1)}, f32[1,4,256]{2,1,0:T(4,128)S(1)}, u32[]{:S(2)}, u32[]{:S(2)}) collective-permute-start(f32[1,4,256]{2,1,0:T(4,128)S(1)} %get-tuple-element.340), channel_id=1, source_target_pairs={{0,3},{1,4},{2,5},{3,6},{4,7},{5,8},{6,9},{7,10},{8,11},{9,12},{10... | collective-permute-start | bytes 12296 | tf_op jit(solution)/shard_map/ppermute | solution.py:19
  137.6 6.3 %collective-permute-start.13 = (f32[1,4,256]{2,1,0:T(4,128)S(1)}, f32[1,4,256]{2,1,0:T(4,128)S(1)}, u32[]{:S(2)}, u32[]{:S(2)}) collective-permute-start(f32[1,4,256]{2,1,0:T(4,128)S(1)} %get-tuple-element.339), channel_id=1, source_target_pairs={{0,2},{1,3},{2,4},{3,5},{4,6},{5,7},{6,8},{7,9},{8,10},{9,11},{10,... | collective-permute-start | bytes 12296 | tf_op jit(solution)/shard_map/ppermute | solution.py:19
  138.4 5.7 %collective-permute-start.14 = (f32[1,4,256]{2,1,0:T(4,128)S(1)}, f32[1,4,256]{2,1,0:T(4,128)S(1)}, u32[]{:S(2)}, u32[]{:S(2)}) collective-permute-start(f32[1,4,256]{2,1,0:T(4,128)S(1)} %get-tuple-element.338), channel_id=1, source_target_pairs={{0,1},{1,2},{2,3},{3,4},{4,5},{5,6},{6,7},{7,8},{8,9},{9,10},{10,1... | collective-permute-start | bytes 12296 | tf_op jit(solution)/shard_map/ppermute | solution.py:19
  147.9 10.4 %all-to-all-start.4 = ((f32[16,4,256]{2,1,0:T(4,128)}), f32[16,4,256]{2,1,0:T(4,128)S(1)}, u32[]{:S(2)}, u32[]{:S(2)}) async-start(f32[16,4,256]{2,1,0:T(4,128)} %reshape.223), calls=%async_computation.4 | async-start | bytes 131072 | tf_op jit(solution)/shard_map/all_to_all | solution.py:145
  182.9 10.7 %collective-permute-start.15 = (f32[1,4,256]{2,1,0:T(4,128)S(1)}, f32[1,4,256]{2,1,0:T(4,128)S(1)}, u32[]{:S(2)}, u32[]{:S(2)}) collective-permute-start(f32[1,4,256]{2,1,0:T(4,128)S(1)} %get-tuple-element.337), channel_id=1, source_target_pairs={{0,15},{1,0},{2,1},{3,2},{4,3},{5,4},{6,5},{7,6},{8,7},{9,8},{10,9... | collective-permute-start | bytes 12296 | tf_op jit(solution)/shard_map/ppermute | solution.py:19
  183.9 13.4 %collective-permute-start.16 = (f32[1,4,256]{2,1,0:T(4,128)S(1)}, f32[1,4,256]{2,1,0:T(4,128)S(1)}, u32[]{:S(2)}, u32[]{:S(2)}) collective-permute-start(f32[1,4,256]{2,1,0:T(4,128)S(1)} %get-tuple-element.336), channel_id=1, source_target_pairs={{0,14},{1,15},{2,0},{3,1},{4,2},{5,3},{6,4},{7,5},{8,6},{9,7},{10,... | collective-permute-start | bytes 12296 | tf_op jit(solution)/shard_map/ppermute | solution.py:19
  185.3 12.1 %collective-permute-start.17 = (f32[1,4,256]{2,1,0:T(4,128)S(1)}, f32[1,4,256]{2,1,0:T(4,128)S(1)}, u32[]{:S(2)}, u32[]{:S(2)}) collective-permute-start(f32[1,4,256]{2,1,0:T(4,128)S(1)} %get-tuple-element.335), channel_id=1, source_target_pairs={{0,13},{1,14},{2,15},{3,0},{4,1},{5,2},{6,3},{7,4},{8,5},{9,6},{10... | collective-permute-start | bytes 12296 | tf_op jit(solution)/shard_map/ppermute | solution.py:19
  185.3 14.5 %collective-permute-start.18 = (f32[1,4,256]{2,1,0:T(4,128)S(1)}, f32[1,4,256]{2,1,0:T(4,128)S(1)}, u32[]{:S(2)}, u32[]{:S(2)}) collective-permute-start(f32[1,4,256]{2,1,0:T(4,128)S(1)} %get-tuple-element.334), channel_id=1, source_target_pairs={{0,12},{1,13},{2,14},{3,15},{4,0},{5,1},{6,2},{7,3},{8,4},{9,5},{1... | collective-permute-start | bytes 12296 | tf_op jit(solution)/shard_map/ppermute | solution.py:19
  186.6 13.7 %collective-permute-start.19 = (f32[1,4,256]{2,1,0:T(4,128)S(1)}, f32[1,4,256]{2,1,0:T(4,128)S(1)}, u32[]{:S(2)}, u32[]{:S(2)}) collective-permute-start(f32[1,4,256]{2,1,0:T(4,128)S(1)} %get-tuple-element.333), channel_id=1, source_target_pairs={{0,11},{1,12},{2,13},{3,14},{4,15},{5,0},{6,1},{7,2},{8,3},{9,4},{... | collective-permute-start | bytes 12296 | tf_op jit(solution)/shard_map/ppermute | solution.py:19
  190.1 25.7 %all-to-all-start.5 = ((f32[16,4,256]{2,1,0:T(4,128)}), f32[16,4,256]{2,1,0:T(4,128)S(1)}, u32[]{:S(2)}, u32[]{:S(2)}) async-start(f32[16,4,256]{2,1,0:T(4,128)} %reshape.231), calls=%async_computation.5 | async-start | bytes 131072 | tf_op jit(solution)/shard_map/all_to_all | solution.py:114
  193.6 9.0 %collective-permute-start.20 = (f32[1,4,256]{2,1,0:T(4,128)S(1)}, f32[1,4,256]{2,1,0:T(4,128)S(1)}, u32[]{:S(2)}, u32[]{:S(2)}) collective-permute-start(f32[1,4,256]{2,1,0:T(4,128)S(1)} %get-tuple-element.332), channel_id=1, source_target_pairs={{0,10},{1,11},{2,12},{3,13},{4,14},{5,15},{6,0},{7,1},{8,2},{9,3},... | collective-permute-start | bytes 12296 | tf_op jit(solution)/shard_map/ppermute | solution.py:19
  197.3 6.3 %collective-permute-start.21 = (f32[1,4,256]{2,1,0:T(4,128)S(1)}, f32[1,4,256]{2,1,0:T(4,128)S(1)}, u32[]{:S(2)}, u32[]{:S(2)}) collective-permute-start(f32[1,4,256]{2,1,0:T(4,128)S(1)} %get-tuple-element.331), channel_id=1, source_target_pairs={{0,9},{1,10},{2,11},{3,12},{4,13},{5,14},{6,15},{7,0},{8,1},{9,2},... | collective-permute-start | bytes 12296 | tf_op jit(solution)/shard_map/ppermute | solution.py:19
  197.4 7.8 %collective-permute-start.22 = (f32[1,4,256]{2,1,0:T(4,128)S(1)}, f32[1,4,256]{2,1,0:T(4,128)S(1)}, u32[]{:S(2)}, u32[]{:S(2)}) collective-permute-start(f32[1,4,256]{2,1,0:T(4,128)S(1)} %get-tuple-element.330), channel_id=1, source_target_pairs={{0,8},{1,9},{2,10},{3,11},{4,12},{5,13},{6,14},{7,15},{8,0},{9,1},... | collective-permute-start | bytes 12296 | tf_op jit(solution)/shard_map/ppermute | solution.py:19
  199.8 7.5 %collective-permute-start.23 = (f32[1,4,256]{2,1,0:T(4,128)S(1)}, f32[1,4,256]{2,1,0:T(4,128)S(1)}, u32[]{:S(2)}, u32[]{:S(2)}) collective-permute-start(f32[1,4,256]{2,1,0:T(4,128)S(1)} %get-tuple-element.329), channel_id=1, source_target_pairs={{0,7},{1,8},{2,9},{3,10},{4,11},{5,12},{6,13},{7,14},{8,15},{9,0},... | collective-permute-start | bytes 12296 | tf_op jit(solution)/shard_map/ppermute | solution.py:19
  200.3 7.7 %collective-permute-start.24 = (f32[1,4,256]{2,1,0:T(4,128)S(1)}, f32[1,4,256]{2,1,0:T(4,128)S(1)}, u32[]{:S(2)}, u32[]{:S(2)}) collective-permute-start(f32[1,4,256]{2,1,0:T(4,128)S(1)} %get-tuple-element.328), channel_id=1, source_target_pairs={{0,6},{1,7},{2,8},{3,9},{4,10},{5,11},{6,12},{7,13},{8,14},{9,15},... | collective-permute-start | bytes 12296 | tf_op jit(solution)/shard_map/ppermute | solution.py:19
  205.1 5.4 %collective-permute-start.27 = (f32[1,4,256]{2,1,0:T(4,128)S(1)}, f32[1,4,256]{2,1,0:T(4,128)S(1)}, u32[]{:S(2)}, u32[]{:S(2)}) collective-permute-start(f32[1,4,256]{2,1,0:T(4,128)S(1)} %get-tuple-element.325), channel_id=1, source_target_pairs={{0,3},{1,4},{2,5},{3,6},{4,7},{5,8},{6,9},{7,10},{8,11},{9,12},{10... | collective-permute-start | bytes 12296 | tf_op jit(solution)/shard_map/ppermute | solution.py:19
  207.2 6.3 %collective-permute-start.28 = (f32[1,4,256]{2,1,0:T(4,128)S(1)}, f32[1,4,256]{2,1,0:T(4,128)S(1)}, u32[]{:S(2)}, u32[]{:S(2)}) collective-permute-start(f32[1,4,256]{2,1,0:T(4,128)S(1)} %get-tuple-element.324), channel_id=1, source_target_pairs={{0,2},{1,3},{2,4},{3,5},{4,6},{5,7},{6,8},{7,9},{8,10},{9,11},{10,... | collective-permute-start | bytes 12296 | tf_op jit(solution)/shard_map/ppermute | solution.py:19
  208.0 5.7 %collective-permute-start.29 = (f32[1,4,256]{2,1,0:T(4,128)S(1)}, f32[1,4,256]{2,1,0:T(4,128)S(1)}, u32[]{:S(2)}, u32[]{:S(2)}) collective-permute-start(f32[1,4,256]{2,1,0:T(4,128)S(1)} %get-tuple-element.323), channel_id=1, source_target_pairs={{0,1},{1,2},{2,3},{3,4},{4,5},{5,6},{6,7},{7,8},{8,9},{9,10},{10,1... | collective-permute-start | bytes 12296 | tf_op jit(solution)/shard_map/ppermute | solution.py:19
  (8 other events, 164.1 us)
